TPU v7x, 32 devices: a whole 2x2x4 slice. The times are simulated.
32 devices in a mesh: outer: 2 (over x), rep: 2 (over core), seq: 8 (over z, y).
Axes of the slice: x: 2, y: 2, z: 4, core: 2. Of those that a mesh axis runs over, the one named last changes fastest.
Arguments:
- tokens: bfloat16 [8, 1536, 8192], P(('outer', 'rep'), 'seq'), parts along dimension 0, may hold values from -6 to 6
- value_weight: bfloat16 [8192, 1024], P('seq'), may hold values from -0.0625 to 0.0625
- value_bias: bfloat16 [1024], replicated, may hold values from -3 to 3
- down_matrices: bfloat16 [32, 8192, 64], P(('outer', 'rep', 'seq')), parts along dimension 0, may hold values from -0.0625 to 0.0625
- up_matrices: bfloat16 [32, 64, 1024], P(('outer', 'rep', 'seq')), parts along dimension 0, may hold values from -0.75 to 0.75
- adapter_of_block: int32 [8], P('outer'), parts along dimension 0, may hold values from 0 to 15
- residency: int32 [32], P('outer'), parts along dimension 0, may hold values from 0 to 15, each once
- block_length: int32 [8], P('outer'), parts along dimension 0, may hold values from 384 to 1536, as said below
Outputs:
- values: bfloat16 [8, 1536, 1024], P(('outer', 'rep'), 'seq'), parts along dimension 0
There are 2 independent parts, one for each index of `outer`. A program takes and returns all parts, laid end to end along the dimension named above; an argument that names none is the same for every part. Nothing has to cross between parts.
Inputs may be any that keep to these rules, and one draw needn't show every extreme that they name: `residency`: every adapter id has its own bank slot. `block_length`: some block of every part is full.
All inputs are finite; a program needn't handle non-finite values.
Results may differ from a plain program's by a relative error of at most 0.0038.
Values may be sent and summed in bfloat16 or wider, within the bound.
A program may use at most 128 MiB of HBM per device.

v0:
```python
import jax
import jax.numpy as jnp
from jax import lax
from jax.sharding import PartitionSpec as P


def from_partner(x, axis, apart):
    return lax.ppermute(x, axis, [(i, i ^ 1 << apart) for i in range(lax.axis_size(axis))])


def spread(block, axis, owner):
    block = jnp.where(lax.axis_index(axis) == owner, block, jnp.zeros_like(block))
    return lax.psum(block, axis)


def low_rank(tokens_of_block, shrink_matrix, expand_matrix):
    shrunk_rows = jnp.dot(
        tokens_of_block, shrink_matrix, preferred_element_type=jnp.float32
    ).astype(jnp.bfloat16)
    return jnp.dot(shrunk_rows, expand_matrix, preferred_element_type=jnp.float32)


def body(
    tokens,
    value_weight,
    value_bias,
    down_matrices,
    up_matrices,
    adapter_of_block,
    residency,
    block_length,
):
    block_count, block_rows, model_width = tokens.shape
    out_width = value_weight.shape[1]
    seq_count = lax.axis_size("seq")
    rep_index = lax.axis_index("rep")
    seq_index = lax.axis_index("seq")
    row_count = block_count * block_rows
    flat_rows = tokens.reshape(row_count, model_width)
    adapter_ids = jnp.arange(residency.shape[0], dtype=jnp.int32)
    bank_slot = jnp.sum(
        jnp.where(adapter_of_block[:, None] == adapter_ids[None, :], residency[None, :], 0), axis=1
    )
    owner_rep = bank_slot // seq_count
    owning_sequence = bank_slot % seq_count
    peer_cache = []

    def peer_tokens():
        peer_cache.append(from_partner(tokens, "rep", 0))
        return peer_cache[0]

    base = jnp.dot(
        flat_rows,
        lax.all_gather(value_weight, "seq", axis=0, tiled=True),
        preferred_element_type=jnp.float32,
    )
    base = base + value_bias.astype(jnp.float32)[None, :]

    def local_term(tokens_of_block, block_number):
        is_local = owner_rep[block_number] == rep_index
        shrink_matrix, expand_matrix = (
            spread(down_matrices, "seq", owning_sequence[block_number]),
            spread(up_matrices, "seq", owning_sequence[block_number]),
        )
        return jnp.where(
            is_local, low_rank(tokens_of_block, shrink_matrix[0], expand_matrix[0]), 0.0
        )

    other_tokens = peer_tokens()
    own_terms = []
    peer_terms = []
    for member in range(block_count):
        own_terms.append(local_term(tokens[member], rep_index * block_count + member))
        peer_terms.append(local_term(other_tokens[member], (1 - rep_index) * block_count + member))
    returned_terms = from_partner(jnp.stack(peer_terms, 0), "rep", 0)
    adapter_update = jnp.stack(own_terms, 0) + returned_terms
    positions = seq_index * block_rows + jnp.arange(block_rows, dtype=jnp.int32)
    own_lengths = lax.dynamic_slice_in_dim(block_length, rep_index * block_count, block_count)
    live = positions[None, :] < own_lengths[:, None]
    total = base.reshape(block_count, block_rows, out_width) + adapter_update
    return jnp.where(live[:, :, None], total, 0.0).astype(jnp.bfloat16)


def solution(mesh):
    in_specs = (
        P(("outer", "rep"), "seq", None),
        P("seq", None),
        P(),
        P(("outer", "rep", "seq"), None, None),
        P(("outer", "rep", "seq"), None, None),
        P("outer"),
        P("outer"),
        P("outer"),
    )
    out_specs = P(("outer", "rep"), "seq", None)
    return jax.shard_map(body, mesh=mesh, in_specs=in_specs, out_specs=out_specs, check_vma=False)
```

profile of v0, /device:TPU:0, one launch (start us, length us, event | category | flops | bytes accessed | tf_op | source)
XLA Modules:
  0.0 439.7 jit_solution(12444701351885883064)
XLA Ops:
  6.5 0.0 all-reduce.3.cloned.1.call-start
  6.5 0.9 select_reduce_fusion
  7.4 0.7 fusion.27
  10.7 1.7 select_bitcast_fusion.7
  12.4 3.3 select_bitcast_fusion.3
  15.7 0.0 all-reduce.3.cloned.1.call-update
  15.7 0.0 all-gather.2.cloned.1.call-start
  15.8 0.7 all-gather.2.cloned.1.call-update
  16.5 0.5 collective-permute-start
  17.0 0.0 copy-done.2
  19.4 0.0 copy-done.8
  19.4 0.1 dynamic_slice.31
  19.5 0.1 broadcast_compare_fusion
  19.5 171.3 %all-reduce.3.cloned.1.call-done = (bf16[64,1024]{1,0:T(8,128)(2,1)}, bf16[8192,64]{0,1:T(8,128)(2,1)}, bf16[64,1024]{1,0:T(8,128)(2,1)}, bf16[8192,64]{0,1:T(8,...) async-done(((bf16[64,1024]{1,0:T(8,128)(2,1)}, bf16[8192,64]{0,1:T(8,128)(2,1)}, ...) | async-done | bytes 4718608 | tf_op jit(solution)/shard_map/psum | solution.py:13
  190.9 4.7 %fusion.13 = f32[1,192,1024]{2,1,0:T(8,128)} fusion(bf16[64,1024]{1,0:T(8,128)(2,1)} %get-tuple-element.9, bf16[8192,64]{0,1:T(8,128)(2,1)} %get-tuple-element.10, bf16[2,192,8192]{2,1,0:T(8,128)(2,1)} %param.8, pred[]{:T(512)S(6)} %eq.48), kind=kOutput, calls=%fused_computation.21 | convolution fusion | flops 226701312 | bytes 5111809 | tf_op jit(solution)/shard_map/dot_general | solution.py:20
  195.6 0.0 copy-done.4
  195.6 0.0 copy-done.7
  195.6 4.5 %fusion.14 = f32[1,192,1024]{2,1,0:T(8,128)} fusion(bf16[64,1024]{1,0:T(8,128)(2,1)S(1)} %copy-done.7, bf16[8192,64]{0,1:T(8,128)(2,1)S(1)} %copy-done.4, bf16[2,192,8192]{2,1,0:T(8,128)(2,1)} %param.8, pred[]{:T(512)S(6)} %eq.46), kind=kOutput, calls=%fused_computation.23 | convolution fusion | flops 226701312 | bytes 5111809 | tf_op jit(solution)/shard_map/dot_general | solution.py:20
  200.1 0.0 collective-permute-done
  200.1 0.0 copy-done.6
  200.1 4.4 %fusion.11 = f32[1,192,1024]{2,1,0:T(8,128)S(1)} fusion(bf16[64,1024]{1,0:T(8,128)(2,1)S(1)} %copy-done.6, bf16[8192,64]{0,1:T(8,128)(2,1)} %get-tuple-element.6, bf16[2,192,8192]{2,1,0:T(8,128)(2,1)} %collective-permute-done, pred[]{:T(512)S(6)} %eq.52), kind=kOutput, calls=%fused_computation.17 | convolution fusion | flops 226701312 | bytes 5111809 | tf_op jit(solution)/shard_map/dot_general | solution.py:20
  204.5 0.0 copy-done.3
  204.5 0.0 copy-done.5
  204.5 3.5 fusion.12
  208.0 0.2 pad_maximum_fusion
  208.2 0.1 collective-permute-start.1
  208.3 211.2 %all-gather.2.cloned.1.call-done = bf16[8192,1024]{1,0:T(8,128)(2,1)} async-done(((bf16[1024,1024]{1,0:T(8,128)(2,1)}), bf16[8192,1024]{1,0:T(8,128)(2,1)}) %all-gather.2.cloned.1.call-update) | async-done | bytes 16777232 | tf_op jit(solution)/shard_map/all_gather | solution.py:54
  419.5 12.1 %convolution_add_fusion = f32[384,1024]{1,0:T(8,128)S(1)} fusion(bf16[384,8192]{1,0:T(8,128)(2,1)} %bitcast.73, bf16[8192,1024]{1,0:T(8,128)(2,1)} %all-gather.2.cloned.1.call-done, f32[1024]{0:T(1024)S(1)} %convert_element_type.22), kind=kOutput, calls=%fused_computation.15 | convolution fusion | flops 6442844160 | bytes 24645632 | tf_op jit(solution)/shard_map/dot_general | solution.py:52
  431.6 0.0 collective-permute-done.1
  431.6 0.0 copy-done
  431.6 0.0 copy-done.1
  431.6 1.2 fusion.10
  (12 shorter events, 0.0 us)
Async XLA Ops:
  6.5 184.3 %all-reduce.3.cloned.1.call-start = ((), (), s32[]{:S(2)}) async-start(), calls=%async_computation.1 | async-start | bytes 9437184 | tf_op jit(solution)/shard_map/psum | solution.py:13
  15.7 1.3 copy-start.2
  15.7 3.7 copy-start.8
  15.7 403.7 %all-gather.2.cloned.1.call-start = ((), (), s32[]{:S(2)}) async-start(), calls=%async_computation | async-start | bytes 18874368 | tf_op jit(solution)/shard_map/all_gather | solution.py:54
  16.5 183.6 %collective-permute-start = (bf16[2,192,8192]{2,1,0:T(8,128)(2,1)}, bf16[2,192,8192]{2,1,0:T(8,128)(2,1)}, u32[]{:S(2)}, u32[]{:S(2)}) collective-permute-start(bf16[2,192,8192]{2,1,0:T(8,128)(2,1)} %param.8), channel_id=1, source_target_pairs={{0,8},{8,0},{1,9},{9,1},{2,10},{10,2},{3,11},{11,3},{4,12},{12,4},... | collective-permute-start | bytes 18874376 | tf_op jit(solution)/shard_map/ppermute | solution.py:8
  190.9 4.7 %copy-start.4 = (bf16[8192,64]{0,1:T(8,128)(2,1)S(1)}, bf16[8192,64]{0,1:T(8,128)(2,1)}, u32[]{:S(2)}) copy-start(bf16[8192,64]{0,1:T(8,128)(2,1)} %get-tuple-element.12) | copy-start | bytes 3145732
  190.9 4.7 %copy-start.7 = (bf16[64,1024]{1,0:T(8,128)(2,1)S(1)}, bf16[64,1024]{1,0:T(8,128)(2,1)}, u32[]{:S(2)}) copy-start(bf16[64,1024]{1,0:T(8,128)(2,1)} %get-tuple-element.11) | copy-start | bytes 393220
  195.6 4.5 %copy-start.6 = (bf16[64,1024]{1,0:T(8,128)(2,1)S(1)}, bf16[64,1024]{1,0:T(8,128)(2,1)}, u32[]{:S(2)}) copy-start(bf16[64,1024]{1,0:T(8,128)(2,1)} %get-tuple-element.5) | copy-start | bytes 393220
  200.1 4.5 %copy-start.3 = (bf16[8192,64]{0,1:T(8,128)(2,1)S(1)}, bf16[8192,64]{0,1:T(8,128)(2,1)}, u32[]{:S(2)}) copy-start(bf16[8192,64]{0,1:T(8,128)(2,1)} %get-tuple-element.8) | copy-start | bytes 3145732
  200.1 4.5 %copy-start.5 = (bf16[64,1024]{1,0:T(8,128)(2,1)S(1)}, bf16[64,1024]{1,0:T(8,128)(2,1)}, u32[]{:S(2)}) copy-start(bf16[64,1024]{1,0:T(8,128)(2,1)} %get-tuple-element.7) | copy-start | bytes 393220
  208.2 223.4 %collective-permute-start.1 = (f32[2,192,1024]{2,1,0:T(8,128)S(1)}, f32[2,192,1024]{2,1,0:T(8,128)S(1)}, u32[]{:S(2)}, u32[]{:S(2)}) collective-permute-start(f32[2,192,1024]{2,1,0:T(8,128)S(1)} %pad_maximum_fusion), channel_id=1, source_target_pairs={{0,8},{8,0},{1,9},{9,1},{2,10},{10,2},{3,11},{11,3},{4,12},{12,4},... | collective-permute-start | bytes 4718600 | tf_op jit(solution)/shard_map/ppermute | solution.py:8
  419.4 12.2 %copy-start = (f32[1,192,1024]{2,1,0:T(8,128)S(1)}, f32[1,192,1024]{2,1,0:T(8,128)}, u32[]{:S(2)}) copy-start(f32[1,192,1024]{2,1,0:T(8,128)} %fusion.13) | copy-start | bytes 2359300
  419.5 12.2 %copy-start.1 = (f32[1,192,1024]{2,1,0:T(8,128)S(1)}, f32[1,192,1024]{2,1,0:T(8,128)}, u32[]{:S(2)}) copy-start(f32[1,192,1024]{2,1,0:T(8,128)} %fusion.14) | copy-start | bytes 2359300
Sparse Core Ops, SparseCore 0:
  15.9 174.9 all-reduce.2
  193.0 226.4 all-gather.1
where the time goes:
time: 440 us
  waiting for transfers between devices  383 us (87%)
  matrix products  29.2 us (7%)
  between operations  18.4 us (4%)
  other arithmetic  7.37 us (2%)
    all_gather x1, waiting for transfers between devices, body(): lax.all_gather(value_weight, 'seq', axis=0, tiled=True)  211 us
    psum x1, waiting for transfers between devices, spread(): return lax.psum(block, axis)  171 us
    dot_general x4, matrix products, low_rank(): jnp.dot(shrunk_rows, expand_matrix, preferred_element_type=jnp.float32)  17.1 us
    dot_general x1, matrix products, body(): jnp.dot(flat_rows, lax.all_gather(value_weight, 'seq', axis=0, tiled=True...  12.1 us
  transfers between devices with their start and end apart: 4, of which 2 were waited for; matrix products, arithmetic and copies ran while one was open for 7% of the time, Pallas kernels for 0%

commit v1 on v0

v1 whole, which is shorter than its diff:
```python
import functools
import jax
import jax.numpy as jnp
from jax import lax
from jax.experimental import pallas as pl
from jax.experimental.pallas import tpu as pltpu
from jax.sharding import PartitionSpec as P

MESH = pl.DeviceIdType.MESH


def grid_of(n):
    near = 1
    while near * near * 4 <= n:
        near *= 2
    return n // near, near


def gather_kernel(
    n, A, B, pick_ref, home_ref, w_ref, bank_ref, w_out, ad_out,
    bank_in, mine, lent, borrowed,
    w_send, w_recv, ad_send, ad_recv, swap_send, swap_recv, lend_sems, local_sems,
):
    o, r, s = lax.axis_index("outer"), lax.axis_index("rep"), lax.axis_index("seq")
    a, b = s // B, s % B
    own, other, sib_own, sib_other = o * 2 + r, (1 - o) * 2 + r, o * 2 + 1 - r, (1 - o) * 2 + 1 - r
    side = {"outer": 1 - o}
    sibling = {"rep": 1 - r}

    barrier = pltpu.get_barrier_semaphore()
    for k in range(1, n):
        pl.semaphore_signal(barrier, inc=1, device_id={"seq": (s + k) % n}, device_id_type=MESH)
    pl.semaphore_signal(barrier, inc=1, device_id=side, device_id_type=MESH)
    pl.semaphore_signal(barrier, inc=1, device_id=sibling, device_id_type=MESH)
    pl.semaphore_wait(barrier, n + 1)

    sent = []

    def start(ok, copy):
        def go():
            copy.start()

        if ok is None:
            go()
        else:
            pl.when(ok)(go)
        sent.append((ok, copy))

    def remote(src, dst, send, recv, device):
        return pltpu.make_async_remote_copy(
            src_ref=src, dst_ref=dst, send_sem=send, recv_sem=recv, device_id=device, device_id_type=MESH
        )

    def both(x, y):
        return x if y is None else (y if x is None else jnp.logical_and(x, y))

    def far(step):
        at = a + step
        ok = jnp.logical_and(at >= 0, at < A)
        return ok, jnp.clip(at, 0, A - 1)

    def near(step):
        at = b + step
        ok = jnp.logical_and(at >= 0, at < B)
        return ok, jnp.clip(at, 0, B - 1)

    class Flow:
        def __init__(self, out, send, recv, wide):
            self.out, self.send, self.recv, self.wide = out, send, recv, wide

        def put(self, ok, src, shard, lane, device):
            start(ok, remote(src, self.out(shard), self.send.at[lane, shard], self.recv(shard), device))

        def far_put(self, ok, src, shard, step):
            there, row = far(step)
            self.put(both(ok, there), src, shard, 0 if step < 0 else 1, {"seq": row * B + b})

        def near_put(self, ok, src, shard, step):
            there, col = near(step)
            self.put(both(ok, there), src, shard, 2 if step < 0 else 3, {"seq": a * B + col})

        def arrive(self, ok, shard):
            block = self.out(shard)

            @pl.when(ok)
            def _():
                pltpu.make_async_copy(block, block, self.recv(shard)).wait()

            return block

        def widen(self, ok, src, shard):
            if self.wide:
                self.put(ok, src, shard, 4, side)
                self.put(ok, src, shard, 5, sibling)

        def begin(self, src):
            for step in (-1, 1):
                self.far_put(None, src, s, step)
            for step in (-1, 1):
                self.near_put(None, src, s, step)

        def wave(self, d):
            rows = []
            for sign in (-1, 1) if d else (1,):
                ok, row = far(sign * d)
                rows.append((ok if d else None, row))
                if d:
                    shard = row * B + b
                    src = self.arrive(ok, shard)
                    self.far_put(ok, src, shard, -sign)
                    for step in (-1, 1):
                        self.near_put(ok, src, shard, step)
                    self.widen(ok, src, shard)
            for row_ok, row in rows:
                for e in range(1, B):
                    for sign in (-1, 1):
                        there, col = near(sign * e)
                        ok = both(row_ok, there)
                        shard = row * B + col
                        src = self.arrive(ok, shard)
                        if e < B - 1:
                            self.near_put(ok, src, shard, -sign)
                        self.widen(ok, src, shard)

        def shards(self, d):
            found = []
            for sign in (-1, 1) if d else (1,):
                row_ok, row = far(sign * d)
                if d:
                    found.append((row_ok, row * B + b))
                for e in range(1, B):
                    for near_sign in (-1, 1):
                        there, col = near(near_sign * e)
                        found.append((both(row_ok if d else None, there), row * B + col))
            return found

    weights = Flow(lambda k: w_out.at[k, own], w_send, lambda k: w_recv.at[own, k], True)
    adapters = Flow(lambda k: ad_out.at[k], ad_send, lambda k: ad_recv.at[k], False)

    def cross(d):
        for ok, shard in weights.shards(d):
            block = w_out.at[shard, other]

            @pl.when(ok)
            def _(block=block, shard=shard):
                pltpu.make_async_copy(block, block, w_recv.at[other, shard]).wait()

            start(ok, remote(block, block, w_send.at[6, shard], w_recv.at[other, shard], sibling))

    for k in range(1, n):
        to = (s + k) % n
        start(None, remote(bank_ref.at[to], bank_in.at[s], swap_send.at[k], swap_recv.at[s], {"seq": to}))
    weights.begin(w_ref.at[own])
    kept = pltpu.make_async_copy(bank_ref.at[s], bank_in.at[s], local_sems.at[0])
    kept.start()
    whole = pltpu.make_async_copy(w_ref, w_out.at[s], local_sems.at[1])
    whole.start()

    weights.wave(0)
    if A > 1:
        weights.wave(1)

    kept.wait()
    for k in range(1, n):
        sender = (s + k) % n
        part = bank_in.at[sender]
        pltpu.make_async_copy(part, part, swap_recv.at[sender]).wait()
    pair = mine.shape[0]
    for c in range(pair):
        lent[c] = bank_in[pick_ref[(1 - r) * pair + c]]
    lend = remote(lent, borrowed, lend_sems.at[0], lend_sems.at[1], sibling)
    lend.start()
    lend.wait()
    for c in range(pair):
        here = home_ref[r * pair + c] == r
        mine[c] = jnp.where(here, bank_in[pick_ref[r * pair + c]], borrowed[c])
    adapters.begin(mine)
    stored = pltpu.make_async_copy(mine, ad_out.at[s], local_sems.at[2])
    stored.start()

    cross(0)
    for d in range(2, A):
        weights.wave(d)
        adapters.wave(d - 2)
        cross(d - 1)
    for d in range(max(A - 2, 0), A):
        adapters.wave(d)
    if A > 1:
        cross(A - 1)
    for k in range(1, n):
        shard = (s + k) % n
        for quarter in (sib_own, sib_other):
            block = w_out.at[shard, quarter]
            pltpu.make_async_copy(block, block, w_recv.at[quarter, shard]).wait()
    whole.wait()
    stored.wait()
    for ok, copy in sent:
        if ok is None:
            copy.wait_send()
        else:
            pl.when(ok)(copy.wait_send)


def gather_all(n, weight, bank, pick, home, pair):
    A, B = grid_of(n)
    quarter_rows, width = weight.shape[0] // 4, weight.shape[1]
    part = bank.shape[1:]
    any_space = pl.BlockSpec(memory_space=pl.ANY)
    scalars = pl.BlockSpec(memory_space=pltpu.SMEM)
    dma = pltpu.SemaphoreType.DMA
    return pl.pallas_call(
        functools.partial(gather_kernel, n, A, B),
        out_shape=(
            jax.ShapeDtypeStruct((n, 4, quarter_rows, width), weight.dtype),
            jax.ShapeDtypeStruct((n, pair) + part, bank.dtype),
        ),
        in_specs=[scalars, scalars, any_space, any_space],
        out_specs=(any_space, any_space),
        scratch_shapes=[
            pltpu.VMEM((n,) + part, bank.dtype),
            pltpu.VMEM((pair,) + part, bank.dtype),
            pltpu.VMEM((pair,) + part, bank.dtype),
            pltpu.VMEM((pair,) + part, bank.dtype),
            dma((7, n)),
            dma((4, n)),
            dma((4, n)),
            dma((n,)),
            dma((n,)),
            dma((n,)),
            dma((2,)),
            dma((3,)),
        ],
        compiler_params=pltpu.CompilerParams(
            collective_id=0, has_side_effects=True, vmem_limit_bytes=24 << 20
        ),
    )(pick, home, weight.reshape(4, quarter_rows, width), bank)


def body(
    tokens,
    value_weight,
    value_bias,
    down_matrices,
    up_matrices,
    adapter_of_block,
    residency,
    block_length,
):
    block_count, block_rows, model_width = tokens.shape
    rank = down_matrices.shape[2]
    out_width = value_weight.shape[1]
    n = lax.axis_size("seq")
    rep_index = lax.axis_index("rep")
    seq_index = lax.axis_index("seq")
    adapter_ids = jnp.arange(residency.shape[0], dtype=jnp.int32)
    bank_slot = jnp.sum(
        jnp.where(adapter_of_block[:, None] == adapter_ids[None, :], residency[None, :], 0), axis=1
    ).astype(jnp.int32)

    fold = 128 // rank
    down_rows = model_width // n // fold
    up_rows = rank * out_width // n // 128
    pad = -(down_rows + up_rows) % 16
    bank = jnp.concatenate(
        [
            down_matrices[0].reshape(n, fold, down_rows, rank).transpose(0, 2, 1, 3).reshape(n, down_rows, 128),
            up_matrices[0].reshape(n, up_rows, 128),
            jnp.zeros((n, pad, 128), down_matrices.dtype),
        ],
        axis=1,
    )
    weight, parts = gather_all(n, value_weight, bank, bank_slot % n, bank_slot // n, block_count)

    base = jnp.dot(
        tokens.reshape(block_count * block_rows, model_width),
        weight.reshape(model_width, out_width),
        preferred_element_type=jnp.float32,
    ).reshape(block_count, block_rows, out_width)
    down = (
        parts[:, :, :down_rows]
        .reshape(n, block_count, down_rows, fold, rank)
        .transpose(1, 0, 3, 2, 4)
        .reshape(block_count, model_width, rank)
    )
    up = parts[:, :, down_rows : down_rows + up_rows].transpose(1, 0, 2, 3).reshape(block_count, rank, out_width)
    shrunk = jnp.einsum("ctk,ckl->ctl", tokens, down, preferred_element_type=jnp.float32).astype(jnp.bfloat16)
    delta = jnp.einsum("ctl,clv->ctv", shrunk, up, preferred_element_type=jnp.float32)
    positions = seq_index * block_rows + jnp.arange(block_rows, dtype=jnp.int32)
    own_lengths = lax.dynamic_slice_in_dim(block_length, rep_index * block_count, block_count)
    live = positions[None, :] < own_lengths[:, None]
    total = base + value_bias.astype(jnp.float32)[None, None, :] + delta
    return jnp.where(live[:, :, None], total, 0.0).astype(jnp.bfloat16)


def solution(mesh):
    in_specs = (
        P(("outer", "rep"), "seq", None),
        P("seq", None),
        P(),
        P(("outer", "rep", "seq"), None, None),
        P(("outer", "rep", "seq"), None, None),
        P("outer"),
        P("outer"),
        P("outer"),
    )
    out_specs = P(("outer", "rep"), "seq", None)
    return jax.shard_map(body, mesh=mesh, in_specs=in_specs, out_specs=out_specs, check_vma=False)
```

time: 440 us -> 161 us (0.37)
  waiting for transfers between devices: 383 us -> 0 us
  Pallas kernels: 0 us -> 125 us
  between operations: 18.4 us -> 0.13 us
  local copies, waits for them, and re-layouts: 0.81 us -> 17 us
  matrix products: 29.2 us -> 16.7 us
  other arithmetic: 7.37 us -> 1.03 us
    all_gather x1 -> x0, waiting for transfers between devices: 211 us -> none  [body(): lax.all_gather(value_weight, 'seq', axis=0, tiled=True)]
    psum x1 -> x0, waiting for transfers between devices: 171 us -> none  [spread(): return lax.psum(block, axis)]
    pallas_call x0 -> x1, Pallas kernels: none -> 125 us  [gather_all(): pl.pallas_call(functools.partial(gather_kernel, n, A, B), out_shape=(jax....]
    dot_general x5 -> x2, matrix products: 29.2 us -> 16.7 us  [the longest x1 10 us: body(): jnp.dot(tokens.reshape(block_count * block_rows, model_width), weight.res...]
    squeeze x2 -> x0, other arithmetic: 5.02 us -> none  [the longest x1 3.33 us: local_term(): shrink_matrix[0]]
  transfers between devices with their start and end apart: 4 -> 0, of which waited for: 2 -> 0; matrix products, arithmetic and copies ran while one was open for 7% -> 0% of each run, Pallas kernels for 0% -> 0%
where the time goes in v1:
time: 161 us; the launch traced here: 160 us
  Pallas kernels  125 us (78%)
  local copies, waits for them, and re-layouts  17 us (11%)
  matrix products  16.7 us (10%)
    pallas_call x1, Pallas kernels, gather_all(): pl.pallas_call(functools.partial(gather_kernel, n, A, B), out_shape=(jax....  125 us
    dot_general x1, matrix products, body(): jnp.dot(tokens.reshape(block_count * block_rows, model_width), weight.res...  10 us
    dot_general x1, matrix products, body(): jnp.einsum('ctl,clv->ctv', shrunk, up, preferred_element_type=jnp.float32)  6.7 us
    slice x2, local copies, waits for them, and re-layouts, body(): parts[:, :, :down_rows].reshape(n, block_count, down_rows, fold, rank)  4.34 us
    transpose x1, local copies, waits for them, and re-layouts, body(): down = parts[:, :, :down_rows].reshape(n, block_count, down_rows, fold, r...  3.53 us
    reshape x1, local copies, waits for them, and re-layouts, body(): down = parts[:, :, :down_rows].reshape(n, block_count, down_rows, fold, r...  3.31 us

profile of v1, /device:TPU:0, one launch (start us, length us, event | category | flops | bytes accessed | tf_op | source)
XLA Modules:
  0.0 159.6 jit_solution(12323723266937011254)
XLA Ops:
  0.0 0.9 select_reduce_fusion
  0.9 1.0 reshape_squeeze.7
  1.8 1.8 %reshape_squeeze.6 = bf16[8,2,512,64]{2,1,0,3:T(2,128)(2,1)S(1)} reshape(bf16[1,8192,64]{1,2,0:T(8,128)(2,1)} %param.11) | data formatting | bytes 2097152 | tf_op jit(solution)/shard_map/reshape;squeeze | solution.py:266
  3.7 0.6 copy.19
  4.3 0.7 copy.20
  4.9 0.0 copy-start
  4.9 0.1 pad_maximum_fusion.bank_ref
  5.0 1.5 copy-done
  6.5 124.7 %shard_map.82 = (bf16[8,4,256,1024]{3,2,1,0:T(8,128)(2,1)S(1)}, bf16[8,2,576,128]{3,2,1,0:T(8,128)(2,1)S(1)}) custom-call(s32[4]{0:T(128)S(1)} %get-tuple-element.10.pick_ref, s32[4]{0:T(128)S(1)} %get-tuple-element.9.home_ref, bf16[4,256,1024]{2,1,0:T(8,128)(2,1)S(1)} %bitcast.24, bf16[8,576,128]{2,1,0:T(8,128)(2,1)S(1)} %pad_maximum_fusion.bank_ref), custom_call_target="tpu_custom_call" | custom-call | tf_op jit(solution)/shard_map/pallas_call | solution.py:211
  131.3 10.0 %fusion = f32[1024,384]{0,1:T(8,128)} fusion(bf16[384,8192]{1,0:T(8,128)(2,1)} %bitcast.27, bf16[8192,1024]{1,0:T(8,128)(2,1)S(1)} %bitcast.25), kind=kOutput, calls=%fused_computation.13 | convolution fusion | flops 6442450944 | bytes 24641536 | tf_op jit(solution)/shard_map/dot_general | solution.py:274
  141.3 0.1 reshape.66
  141.5 1.5 slice.6
  142.9 2.9 %copy.21 = bf16[8,2,512,128]{2,3,1,0:T(8,128)(2,1)S(1)} copy(bf16[8,2,512,128]{3,2,1,0:T(8,128)(2,1)} %slice.6) | data formatting | bytes 4194304 | tf_op jit(solution)/shard_map/slice | solution.py:280
  145.8 3.5 %copy.22 = bf16[2,8,2,512,64]{3,2,1,4,0:T(2,128)(2,1)} copy(bf16[2,8,2,512,64]{3,4,2,0,1:T(8,128)(2,1)S(1)} %bitcast.26) | data formatting | bytes 4194304 | tf_op jit(solution)/shard_map/transpose | solution.py:282
  149.3 0.0 copy-start.1
  149.3 0.0 copy-start.2
  149.3 3.3 %reshape.65 = bf16[2,8192,64]{1,2,0:T(8,128)(2,1)S(1)} reshape(bf16[2,8,2,512,64]{3,2,1,4,0:T(2,128)(2,1)} %copy.22) | data formatting | bytes 4194304 | tf_op jit(solution)/shard_map/reshape | solution.py:283
  152.7 0.0 copy-done.1
  152.7 0.0 copy-done.2
  152.7 0.1 dynamic_slice.3
  152.8 0.1 broadcast_compare_fusion
  152.9 6.7 %select_convert_fusion = bf16[2,192,1024]{2,1,0:T(8,128)(2,1)} fusion(f32[2,192,1024]{2,1,0:T(8,128)} %bitcast.30, bf16[2,64,1024]{2,1,0:T(8,128)(2,1)S(1)} %reshape.66, bf16[2,8192,64]{1,2,0:T(8,128)(2,1)S(1)} %reshape.65, bf16[2,192,8192]{2,1,0:T(8,128)(2,1)} %param.8, f32[1024]{0:T(1024)S(1)} %convert_element_type.10, ...), kind=kOutput, calls=%fused_computation | convolution fusion | flops 454582272 | bytes 11014528 | tf_op jit(solution)/shard_map/ctl,clv->ctv/dot_general | solution.py:287
  (5 shorter events, 0.1 us)
Async XLA Ops:
  4.9 1.6 copy-start
  149.3 3.3 %copy-start.1 = (bf16[1024]{0:T(1024)(128)(2,1)S(1)}, bf16[1024]{0:T(1024)(128)(2,1)}, u32[]{:S(2)}) copy-start(bf16[1024]{0:T(1024)(128)(2,1)} %param.10) | copy-start | bytes 6148
  149.3 3.4 %copy-start.2 = (s32[4]{0:T(128)S(1)}, s32[4]{0:T(128)}, u32[]{:S(2)}) copy-start(s32[4]{0:T(128)} %param.15) | copy-start | bytes 52

commit v2 on v1

--- a/solution.py
+++ b/solution.py
@@ -17,8 +17,8 @@
 
 
 def gather_kernel(
-    n, A, B, pick_ref, home_ref, w_ref, bank_ref, w_out, ad_out,
-    bank_in, mine, lent, borrowed,
+    n, A, B, rank, pick_ref, home_ref, length_ref, bias_ref, w_ref, bank_ref, tok_ref, out_ref,
+    w_out, ad_out, tok, acc, low, bank_in, mine, lent, borrowed,
     w_send, w_recv, ad_send, ad_recv, swap_send, swap_recv, lend_sems, local_sems,
 ):
     o, r, s = lax.axis_index("outer"), lax.axis_index("rep"), lax.axis_index("seq")
@@ -147,6 +147,58 @@
 
             start(ok, remote(block, block, w_send.at[6, shard], w_recv.at[other, shard], sibling))
 
+    pair, depth, width = mine.shape[0], tok.shape[1] // n, acc.shape[1]
+    block_rows = tok.shape[0] // pair
+    fold = 128 // rank
+    down_rows = depth // fold
+    groups = width // 128
+    tile = min(width, 256)
+
+    def columns(shard):
+        return pl.ds(pl.multiple_of(shard * depth, 128), depth)
+
+    def project(shard, first=False):
+        @pl.loop(0, width // tile)
+        def _(i):
+            at = pl.ds(pl.multiple_of(i * tile, tile), tile)
+            term = jnp.dot(
+                tok[:, columns(shard)],
+                w_out[shard, :, :, at].reshape(depth, tile),
+                preferred_element_type=jnp.float32,
+            )
+            acc[:, at] = term + (bias_ref[:, at].astype(jnp.float32) if first else acc[:, at])
+
+    def reach(d):
+        return 1 + jnp.minimum(a, d) + jnp.minimum(A - 1 - a, d)
+
+    def projects(d):
+        low_end = B * reach(d - 1) if d else 1
+
+        @pl.loop(low_end, B * reach(d))
+        def _(j):
+            k = j // B
+            edge = jnp.minimum(a, A - 1 - a)
+            swing = jnp.where(k % 2 == 1, a - (k + 1) // 2, a + k // 2)
+            row = jnp.where(k <= 2 * edge, swing, jnp.where(2 * a < A, k, A - 1 - k))
+            shard = row * B + (b + j % B) % B
+            for quarter in (sib_own, sib_other):
+                block = w_out.at[shard, quarter]
+                pltpu.make_async_copy(block, block, w_recv.at[quarter, shard]).wait()
+            project(shard)
+
+    def shrink():
+        low[...] = jnp.zeros_like(low)
+
+        @pl.loop(0, n)
+        def _(k):
+            for c in range(pair):
+                rows = tok[c * block_rows : (c + 1) * block_rows, columns(k)]
+                down = ad_out[k, c, :down_rows]
+                for f in range(fold):
+                    low[c, f] += jnp.dot(
+                        rows[:, f * down_rows : (f + 1) * down_rows], down, preferred_element_type=jnp.float32
+                    )
+
     for k in range(1, n):
         to = (s + k) % n
         start(None, remote(bank_ref.at[to], bank_in.at[s], swap_send.at[k], swap_recv.at[s], {"seq": to}))
@@ -155,7 +207,12 @@
     kept.start()
     whole = pltpu.make_async_copy(w_ref, w_out.at[s], local_sems.at[1])
     whole.start()
-
+    held = pltpu.make_async_copy(tok_ref, tok, local_sems.at[3])
+    held.start()
+
+    whole.wait()
+    held.wait()
+    project(s, True)
     weights.wave(0)
     if A > 1:
         weights.wave(1)
@@ -165,7 +222,6 @@
         sender = (s + k) % n
         part = bank_in.at[sender]
         pltpu.make_async_copy(part, part, swap_recv.at[sender]).wait()
-    pair = mine.shape[0]
     for c in range(pair):
         lent[c] = bank_in[pick_ref[(1 - r) * pair + c]]
     lend = remote(lent, borrowed, lend_sems.at[0], lend_sems.at[1], sibling)
@@ -183,17 +239,30 @@
         weights.wave(d)
         adapters.wave(d - 2)
         cross(d - 1)
+        projects(d - 2)
     for d in range(max(A - 2, 0), A):
         adapters.wave(d)
     if A > 1:
+        projects(A - 2)
+    stored.wait()
+    shrink()
+    if A > 1:
         cross(A - 1)
-    for k in range(1, n):
-        shard = (s + k) % n
-        for quarter in (sib_own, sib_other):
-            block = w_out.at[shard, quarter]
-            pltpu.make_async_copy(block, block, w_recv.at[quarter, shard]).wait()
-    whole.wait()
-    stored.wait()
+    projects(A - 1)
+
+    for c in range(pair):
+        rows = slice(c * block_rows, (c + 1) * block_rows)
+        narrow = sum(low[c, f][:, f * rank : (f + 1) * rank] for f in range(fold)).astype(jnp.bfloat16)
+        at = s * block_rows + lax.broadcasted_iota(jnp.int32, (block_rows, 128), 0)
+        live = at < length_ref[r * pair + c]
+        for g in range(groups):
+            pieces = [ad_out[k, c, down_rows : down_rows + rank * groups // n] for k in range(g, n, groups)]
+            up = pieces[0]
+            if len(pieces) > 1:
+                up = jnp.concatenate([x.astype(jnp.float32) for x in pieces], axis=0).astype(jnp.bfloat16)
+            delta = jnp.dot(narrow, up, preferred_element_type=jnp.float32)
+            cut = slice(g * 128, (g + 1) * 128)
+            out_ref[rows, cut] = jnp.where(live, acc[rows, cut] + delta, 0.0).astype(out_ref.dtype)
     for ok, copy in sent:
         if ok is None:
             copy.wait_send()
@@ -201,22 +270,26 @@
             pl.when(ok)(copy.wait_send)
 
 
-def gather_all(n, weight, bank, pick, home, pair):
+def run(n, tokens, weight, bias, bank, pick, home, length, pair, rank):
     A, B = grid_of(n)
     quarter_rows, width = weight.shape[0] // 4, weight.shape[1]
     part = bank.shape[1:]
+    rows = tokens.shape[0]
     any_space = pl.BlockSpec(memory_space=pl.ANY)
     scalars = pl.BlockSpec(memory_space=pltpu.SMEM)
+    vmem = pl.BlockSpec(memory_space=pltpu.VMEM)
     dma = pltpu.SemaphoreType.DMA
     return pl.pallas_call(
-        functools.partial(gather_kernel, n, A, B),
-        out_shape=(
-            jax.ShapeDtypeStruct((n, 4, quarter_rows, width), weight.dtype),
-            jax.ShapeDtypeStruct((n, pair) + part, bank.dtype),
-        ),
-        in_specs=[scalars, scalars, any_space, any_space],
-        out_specs=(any_space, any_space),
+        functools.partial(gather_kernel, n, A, B, rank),
+        out_shape=jax.ShapeDtypeStruct((rows, width), jnp.bfloat16),
+        in_specs=[scalars, scalars, scalars, vmem, any_space, any_space, any_space],
+        out_specs=vmem,
         scratch_shapes=[
+            pltpu.VMEM((n, 4, quarter_rows, width), weight.dtype),
+            pltpu.VMEM((n, pair) + part, bank.dtype),
+            pltpu.VMEM(tokens.shape, tokens.dtype),
+            pltpu.VMEM((rows, width), jnp.float32),
+            pltpu.VMEM((pair, 128 // rank, rows // pair, 128), jnp.float32),
             pltpu.VMEM((n,) + part, bank.dtype),
             pltpu.VMEM((pair,) + part, bank.dtype),
             pltpu.VMEM((pair,) + part, bank.dtype),
@@ -228,12 +301,12 @@
             dma((n,)),
             dma((n,)),
             dma((2,)),
-            dma((3,)),
+            dma((4,)),
         ],
         compiler_params=pltpu.CompilerParams(
-            collective_id=0, has_side_effects=True, vmem_limit_bytes=24 << 20
+            collective_id=0, has_side_effects=True, vmem_limit_bytes=44 << 20
         ),
-    )(pick, home, weight.reshape(4, quarter_rows, width), bank)
+    )(pick, home, length, bias, weight.reshape(4, quarter_rows, width), bank, tokens)
 
 
 def body(
@@ -250,8 +323,6 @@
     rank = down_matrices.shape[2]
     out_width = value_weight.shape[1]
     n = lax.axis_size("seq")
-    rep_index = lax.axis_index("rep")
-    seq_index = lax.axis_index("seq")
     adapter_ids = jnp.arange(residency.shape[0], dtype=jnp.int32)
     bank_slot = jnp.sum(
         jnp.where(adapter_of_block[:, None] == adapter_ids[None, :], residency[None, :], 0), axis=1
@@ -259,37 +330,30 @@
 
     fold = 128 // rank
     down_rows = model_width // n // fold
-    up_rows = rank * out_width // n // 128
+    groups = out_width // 128
+    up_rows = rank * groups // n
     pad = -(down_rows + up_rows) % 16
     bank = jnp.concatenate(
         [
             down_matrices[0].reshape(n, fold, down_rows, rank).transpose(0, 2, 1, 3).reshape(n, down_rows, 128),
-            up_matrices[0].reshape(n, up_rows, 128),
+            up_matrices[0].reshape(n // groups, up_rows, groups, 128).transpose(0, 2, 1, 3).reshape(n, up_rows, 128),
             jnp.zeros((n, pad, 128), down_matrices.dtype),
         ],
         axis=1,
     )
-    weight, parts = gather_all(n, value_weight, bank, bank_slot % n, bank_slot // n, block_count)
-
-    base = jnp.dot(
+    out = run(
+        n,
         tokens.reshape(block_count * block_rows, model_width),
-        weight.reshape(model_width, out_width),
-        preferred_element_type=jnp.float32,
-    ).reshape(block_count, block_rows, out_width)
-    down = (
-        parts[:, :, :down_rows]
-        .reshape(n, block_count, down_rows, fold, rank)
-        .transpose(1, 0, 3, 2, 4)
-        .reshape(block_count, model_width, rank)
+        value_weight,
+        value_bias.reshape(1, out_width),
+        bank,
+        bank_slot % n,
+        bank_slot // n,
+        block_length,
+        block_count,
+        rank,
     )
-    up = parts[:, :, down_rows : down_rows + up_rows].transpose(1, 0, 2, 3).reshape(block_count, rank, out_width)
-    shrunk = jnp.einsum("ctk,ckl->ctl", tokens, down, preferred_element_type=jnp.float32).astype(jnp.bfloat16)
-    delta = jnp.einsum("ctl,clv->ctv", shrunk, up, preferred_element_type=jnp.float32)
-    positions = seq_index * block_rows + jnp.arange(block_rows, dtype=jnp.int32)
-    own_lengths = lax.dynamic_slice_in_dim(block_length, rep_index * block_count, block_count)
-    live = positions[None, :] < own_lengths[:, None]
-    total = base + value_bias.astype(jnp.float32)[None, None, :] + delta
-    return jnp.where(live[:, :, None], total, 0.0).astype(jnp.bfloat16)
+    return out.reshape(block_count, block_rows, out_width)
 
 
 def solution(mesh):

time: 161 us -> 152 us (0.944); the launches traced: 160 us -> 149 us
  matrix products: 16.7 us -> 0 us
  Pallas kernels: 125 us -> 139 us
  local copies, waits for them, and re-layouts: 17 us -> 8.88 us
    dot_general x2 -> x0, matrix products: 16.7 us -> none  [the longest x1 10 us: body(): jnp.dot(tokens.reshape(block_count * block_rows, model_width), weight.res...]
    pallas_call x1, Pallas kernels: 125 us -> 139 us  [run(): pl.pallas_call(functools.partial(gather_kernel, n, A, B, rank), out_shape...]
    slice x2 -> x0, local copies, waits for them, and re-layouts: 4.34 us -> none  [body(): parts[:, :, :down_rows].reshape(n, block_count, down_rows, fold, rank)]
    transpose x3 -> x0, local copies, waits for them, and re-layouts: 3.56 us -> none  [the longest x1 3.53 us: body(): down = parts[:, :, :down_rows].reshape(n, block_count, down_rows, fold, r...]
    reshape x2, local copies, waits for them, and re-layouts: 3.43 us -> 0.03 us  [the longest x1 0.02 us: body(): up_matrices[0].reshape(n // groups, up_rows, groups, 128)]
    unnamed x6 -> x11, local copies, waits for them, and re-layouts: 1.51 us -> 3.68 us
where the time goes in v2:
time: 152 us; the launch traced here: 149 us
  Pallas kernels  139 us (91%)
  local copies, waits for them, and re-layouts  8.88 us (6%)
    pallas_call x1, Pallas kernels, run(): pl.pallas_call(functools.partial(gather_kernel, n, A, B, rank), out_shape...  139 us
    unnamed x11, local copies, waits for them, and re-layouts  3.68 us

profile of v2, /device:TPU:0, one launch (start us, length us, event | category | flops | bytes accessed | tf_op | source)
XLA Modules:
  0.0 148.6 jit_solution(5895480936857330841)
XLA Ops:
  0.0 0.0 copy-start
  0.0 0.9 select_reduce_fusion
  0.9 1.8 %reshape_squeeze.6 = bf16[8,2,512,64]{2,1,0,3:T(2,128)(2,1)S(1)} reshape(bf16[1,8192,64]{1,2,0:T(8,128)(2,1)} %param.11) | data formatting | bytes 2097152 | tf_op jit(solution)/shard_map/reshape;squeeze | solution.py:338
  2.7 1.5 %copy.15 = bf16[8,512,2,64]{1,3,2,0:T(8,128)(2,1)} copy(bf16[8,512,2,64]{1,2,0,3:T(2,128)(2,1)S(1)} %bitcast.20) | data formatting | bytes 2097152 | tf_op jit(solution)/shard_map/transpose | solution.py:338
  4.3 0.0 copy-start.4
  4.3 0.0 copy-start.2
  4.3 0.0 copy-start.3
  4.3 1.8 %copy.17 = bf16[8,512,128]{2,1,0:T(8,128)(2,1)S(1)} copy(bf16[8,512,128]{1,2,0:T(8,128)(2,1)} %bitcast.19) | data formatting | bytes 2097152 | tf_op jit(solution)/shard_map/reshape | solution.py:338
  6.1 0.0 copy-done
  6.1 0.1 pad_maximum_fusion.bank_ref
  6.2 0.0 copy-done.4
  6.3 0.0 copy-done.2
  6.3 0.0 copy-done.3
  6.3 0.0 copy-start.1
  6.3 2.8 %copy-done.1 = bf16[2,192,8192]{2,1,0:T(8,128)(2,1)S(1)} copy-done((bf16[2,192,8192]{2,1,0:T(8,128)(2,1)S(1)}, bf16[2,192,8192]{2,1,0:T(8,128)(2,1)}, u32[]{:S(2)}) %copy-start.1) | copy-done | bytes 6291480
  9.1 138.7 %shard_map.82 = bf16[384,1024]{1,0:T(8,128)(2,1)S(1)} custom-call(s32[4]{0:T(128)S(1)} %get-tuple-element.6.pick_ref, s32[4]{0:T(128)S(1)} %get-tuple-element.5.home_ref, s32[4]{0:T(128)S(1)} %copy-done.3, bf16[1,1024]{1,0:T(2,128)(2,1)S(1)} %reshape.20.bias_ref, bf16[4,256,1024]{2,1,0:T(8,128)(2,1)S(1)} %bitcast.18, ...), custom_call_target="tpu_custom_call" | custom-call | tf_op jit(solution)/shard_map/pallas_call | solution.py:282
  147.7 0.9 copy.21
  (3 shorter events, 0.0 us)
Async XLA Ops:
  0.0 6.1 %copy-start = (bf16[1,64,1024]{2,1,0:T(8,128)(2,1)S(1)}, bf16[1,64,1024]{2,1,0:T(8,128)(2,1)}, u32[]{:S(2)}) copy-start(bf16[1,64,1024]{2,1,0:T(8,128)(2,1)} %param.12) | copy-start | bytes 393220
  4.3 1.9 %copy-start.4 = (bf16[1024]{0:T(1024)(128)(2,1)S(1)}, bf16[1024]{0:T(1024)(128)(2,1)}, u32[]{:S(2)}) copy-start(bf16[1024]{0:T(1024)(128)(2,1)} %param.10) | copy-start | bytes 6148
  4.3 2.0 %copy-start.2 = (bf16[1024,1024]{1,0:T(8,128)(2,1)S(1)}, bf16[1024,1024]{1,0:T(8,128)(2,1)}, u32[]{:S(2)}) copy-start(bf16[1024,1024]{1,0:T(8,128)(2,1)} %param.9) | copy-start | bytes 6291460
  4.3 2.0 %copy-start.3 = (s32[4]{0:T(128)S(1)}, s32[4]{0:T(128)}, u32[]{:S(2)}) copy-start(s32[4]{0:T(128)} %length_ref.1) | copy-start | bytes 52
  6.3 2.8 %copy-start.1 = (bf16[2,192,8192]{2,1,0:T(8,128)(2,1)S(1)}, bf16[2,192,8192]{2,1,0:T(8,128)(2,1)}, u32[]{:S(2)}) copy-start(bf16[2,192,8192]{2,1,0:T(8,128)(2,1)} %param.8) | copy-start | bytes 18874372

commit v3 on v2

--- a/solution.py
+++ b/solution.py
@@ -7,6 +7,7 @@
 from jax.sharding import PartitionSpec as P
 
 MESH = pl.DeviceIdType.MESH
+SLICE_ROWS = 256
 
 
 def grid_of(n):
@@ -17,7 +18,7 @@
 
 
 def gather_kernel(
-    n, A, B, rank, pick_ref, home_ref, length_ref, bias_ref, w_ref, bank_ref, tok_ref, out_ref,
+    n, A, B, S, rank, pick_ref, home_ref, length_ref, bias_ref, w_ref, bank_ref, tok_ref, out_ref,
     w_out, ad_out, tok, acc, low, bank_in, mine, lent, borrowed,
     w_send, w_recv, ad_send, ad_recv, swap_send, swap_recv, lend_sems, local_sems,
 ):
@@ -34,17 +35,19 @@
     pl.semaphore_signal(barrier, inc=1, device_id=sibling, device_id_type=MESH)
     pl.semaphore_wait(barrier, n + 1)
 
-    sent = []
-
-    def start(ok, copy):
+    closing = []
+
+    def start(ok, make, p):
         def go():
-            copy.start()
+            if closing:
+                make(p).wait_send()
+            else:
+                make(p).start()
 
         if ok is None:
             go()
         else:
             pl.when(ok)(go)
-        sent.append((ok, copy))
 
     def remote(src, dst, send, recv, device):
         return pltpu.make_async_remote_copy(
@@ -65,62 +68,68 @@
         return ok, jnp.clip(at, 0, B - 1)
 
     class Flow:
-        def __init__(self, out, send, recv, wide):
-            self.out, self.send, self.recv, self.wide = out, send, recv, wide
-
-        def put(self, ok, src, shard, lane, device):
-            start(ok, remote(src, self.out(shard), self.send.at[lane, shard], self.recv(shard), device))
-
-        def far_put(self, ok, src, shard, step):
+        def __init__(self, out, send, recv, wide, slices):
+            self.out, self.send, self.recv, self.wide, self.slices = out, send, recv, wide, slices
+
+        def put(self, ok, src, shard, lane, device, p):
+            def make(q):
+                return remote(src(q), self.out(shard, q), self.send.at[lane, shard, q], self.recv(shard, q), device)
+
+            start(ok, make, p)
+
+        def far_put(self, ok, src, shard, step, p):
             there, row = far(step)
-            self.put(both(ok, there), src, shard, 0 if step < 0 else 1, {"seq": row * B + b})
-
-        def near_put(self, ok, src, shard, step):
+            self.put(both(ok, there), src, shard, 0 if step < 0 else 1, {"seq": row * B + b}, p)
+
+        def near_put(self, ok, src, shard, step, p):
             there, col = near(step)
-            self.put(both(ok, there), src, shard, 2 if step < 0 else 3, {"seq": a * B + col})
-
-        def arrive(self, ok, shard):
-            block = self.out(shard)
-
-            @pl.when(ok)
-            def _():
-                pltpu.make_async_copy(block, block, self.recv(shard)).wait()
-
-            return block
-
-        def widen(self, ok, src, shard):
+            self.put(both(ok, there), src, shard, 2 if step < 0 else 3, {"seq": a * B + col}, p)
+
+        def arrive(self, ok, shard, p):
+            if not closing:
+
+                @pl.when(ok)
+                def _():
+                    block = self.out(shard, p)
+                    pltpu.make_async_copy(block, block, self.recv(shard, p)).wait()
+
+            return lambda q: self.out(shard, q)
+
+        def widen(self, ok, src, shard, p):
             if self.wide:
-                self.put(ok, src, shard, 4, side)
-                self.put(ok, src, shard, 5, sibling)
+                self.put(ok, src, shard, 4, side, p)
+                self.put(ok, src, shard, 5, sibling, p)
 
         def begin(self, src):
-            for step in (-1, 1):
-                self.far_put(None, src, s, step)
-            for step in (-1, 1):
-                self.near_put(None, src, s, step)
-
-        def wave(self, d):
+            @pl.loop(0, self.slices)
+            def _(p):
+                for step in (-1, 1):
+                    self.far_put(None, src, s, step, p)
+                for step in (-1, 1):
+                    self.near_put(None, src, s, step, p)
+
+        def wave(self, d, p):
             rows = []
             for sign in (-1, 1) if d else (1,):
                 ok, row = far(sign * d)
                 rows.append((ok if d else None, row))
                 if d:
                     shard = row * B + b
-                    src = self.arrive(ok, shard)
-                    self.far_put(ok, src, shard, -sign)
+                    src = self.arrive(ok, shard, p)
+                    self.far_put(ok, src, shard, -sign, p)
                     for step in (-1, 1):
-                        self.near_put(ok, src, shard, step)
-                    self.widen(ok, src, shard)
+                        self.near_put(ok, src, shard, step, p)
+                    self.widen(ok, src, shard, p)
             for row_ok, row in rows:
                 for e in range(1, B):
                     for sign in (-1, 1):
                         there, col = near(sign * e)
                         ok = both(row_ok, there)
                         shard = row * B + col
-                        src = self.arrive(ok, shard)
+                        src = self.arrive(ok, shard, p)
                         if e < B - 1:
-                            self.near_put(ok, src, shard, -sign)
-                        self.widen(ok, src, shard)
+                            self.near_put(ok, src, shard, -sign, p)
+                        self.widen(ok, src, shard, p)
 
         def shards(self, d):
             found = []
@@ -134,18 +143,42 @@
                         found.append((both(row_ok if d else None, there), row * B + col))
             return found
 
-    weights = Flow(lambda k: w_out.at[k, own], w_send, lambda k: w_recv.at[own, k], True)
-    adapters = Flow(lambda k: ad_out.at[k], ad_send, lambda k: ad_recv.at[k], False)
-
-    def cross(d):
+    slice_rows = w_out.shape[2] // S
+
+    def cut(ref, p):
+        return ref.at[pl.ds(p * slice_rows, slice_rows)]
+
+    weights = Flow(
+        lambda k, p: cut(w_out.at[k, own], p), w_send, lambda k, p: w_recv.at[own, k, p], True, S
+    )
+    adapters = Flow(lambda k, p: ad_out.at[k, p], ad_send, lambda k, p: ad_recv.at[k, p], False, mine.shape[0])
+
+    def cross(d, p):
         for ok, shard in weights.shards(d):
-            block = w_out.at[shard, other]
-
-            @pl.when(ok)
-            def _(block=block, shard=shard):
-                pltpu.make_async_copy(block, block, w_recv.at[other, shard]).wait()
-
-            start(ok, remote(block, block, w_send.at[6, shard], w_recv.at[other, shard], sibling))
+
+            if not closing:
+
+                @pl.when(ok)
+                def _(shard=shard):
+                    block = cut(w_out.at[shard, other], p)
+                    pltpu.make_async_copy(block, block, w_recv.at[other, shard, p]).wait()
+
+            def make(q, shard=shard):
+                block = cut(w_out.at[shard, other], q)
+                return remote(block, block, w_send.at[6, shard, q], w_recv.at[other, shard, q], sibling)
+
+            start(ok, make, p)
+
+    def steps(flow, *ds):
+        @pl.loop(0, flow.slices)
+        def _(p):
+            for d in ds:
+                flow.wave(d, p)
+
+    def crosses(d):
+        @pl.loop(0, S)
+        def _(p):
+            cross(d, p)
 
     pair, depth, width = mine.shape[0], tok.shape[1] // n, acc.shape[1]
     block_rows = tok.shape[0] // pair
@@ -182,8 +215,9 @@
             row = jnp.where(k <= 2 * edge, swing, jnp.where(2 * a < A, k, A - 1 - k))
             shard = row * B + (b + j % B) % B
             for quarter in (sib_own, sib_other):
-                block = w_out.at[shard, quarter]
-                pltpu.make_async_copy(block, block, w_recv.at[quarter, shard]).wait()
+                for p in range(S):
+                    block = cut(w_out.at[shard, quarter], p)
+                    pltpu.make_async_copy(block, block, w_recv.at[quarter, shard, p]).wait()
             project(shard)
 
     def shrink():
@@ -199,23 +233,26 @@
                         rows[:, f * down_rows : (f + 1) * down_rows], down, preferred_element_type=jnp.float32
                     )
 
-    for k in range(1, n):
-        to = (s + k) % n
-        start(None, remote(bank_ref.at[to], bank_in.at[s], swap_send.at[k], swap_recv.at[s], {"seq": to}))
-    weights.begin(w_ref.at[own])
+    weights.begin(lambda p: cut(w_ref.at[own], p))
+    whole = pltpu.make_async_copy(w_ref, w_out.at[s], local_sems.at[1])
+    whole.start()
     kept = pltpu.make_async_copy(bank_ref.at[s], bank_in.at[s], local_sems.at[0])
     kept.start()
-    whole = pltpu.make_async_copy(w_ref, w_out.at[s], local_sems.at[1])
-    whole.start()
     held = pltpu.make_async_copy(tok_ref, tok, local_sems.at[3])
     held.start()
 
+    def swap(k):
+        to = (s + k) % n
+        return remote(bank_ref.at[to], bank_in.at[s], swap_send.at[k], swap_recv.at[s], {"seq": to})
+
+    @pl.loop(1, n)
+    def _(k):
+        swap(k).start()
+
+    steps(weights, *range(min(2, A)))
     whole.wait()
     held.wait()
     project(s, True)
-    weights.wave(0)
-    if A > 1:
-        weights.wave(1)
 
     kept.wait()
     for k in range(1, n):
@@ -230,24 +267,23 @@
     for c in range(pair):
         here = home_ref[r * pair + c] == r
         mine[c] = jnp.where(here, bank_in[pick_ref[r * pair + c]], borrowed[c])
-    adapters.begin(mine)
+    adapters.begin(lambda p: mine.at[p])
     stored = pltpu.make_async_copy(mine, ad_out.at[s], local_sems.at[2])
     stored.start()
 
-    cross(0)
+    crosses(0)
     for d in range(2, A):
-        weights.wave(d)
-        adapters.wave(d - 2)
-        cross(d - 1)
+        steps(weights, d)
+        steps(adapters, d - 2)
+        crosses(d - 1)
         projects(d - 2)
-    for d in range(max(A - 2, 0), A):
-        adapters.wave(d)
+    steps(adapters, *range(max(A - 2, 0), A))
     if A > 1:
         projects(A - 2)
     stored.wait()
     shrink()
     if A > 1:
-        cross(A - 1)
+        crosses(A - 1)
     projects(A - 1)
 
     for c in range(pair):
@@ -261,18 +297,26 @@
             if len(pieces) > 1:
                 up = jnp.concatenate([x.astype(jnp.float32) for x in pieces], axis=0).astype(jnp.bfloat16)
             delta = jnp.dot(narrow, up, preferred_element_type=jnp.float32)
-            cut = slice(g * 128, (g + 1) * 128)
-            out_ref[rows, cut] = jnp.where(live, acc[rows, cut] + delta, 0.0).astype(out_ref.dtype)
-    for ok, copy in sent:
-        if ok is None:
-            copy.wait_send()
-        else:
-            pl.when(ok)(copy.wait_send)
+            span = slice(g * 128, (g + 1) * 128)
+            out_ref[rows, span] = jnp.where(live, acc[rows, span] + delta, 0.0).astype(out_ref.dtype)
+
+    @pl.loop(1, n)
+    def _(k):
+        swap(k).wait_send()
+
+    closing.append(True)
+    weights.begin(lambda p: cut(w_ref.at[own], p))
+    adapters.begin(lambda p: mine.at[p])
+    steps(weights, *range(A))
+    steps(adapters, *range(A))
+    for d in range(A):
+        crosses(d)
 
 
 def run(n, tokens, weight, bias, bank, pick, home, length, pair, rank):
     A, B = grid_of(n)
     quarter_rows, width = weight.shape[0] // 4, weight.shape[1]
+    S = max(1, quarter_rows // SLICE_ROWS)
     part = bank.shape[1:]
     rows = tokens.shape[0]
     any_space = pl.BlockSpec(memory_space=pl.ANY)
@@ -280,7 +324,7 @@
     vmem = pl.BlockSpec(memory_space=pltpu.VMEM)
     dma = pltpu.SemaphoreType.DMA
     return pl.pallas_call(
-        functools.partial(gather_kernel, n, A, B, rank),
+        functools.partial(gather_kernel, n, A, B, S, rank),
         out_shape=jax.ShapeDtypeStruct((rows, width), jnp.bfloat16),
         in_specs=[scalars, scalars, scalars, vmem, any_space, any_space, any_space],
         out_specs=vmem,
@@ -294,10 +338,10 @@
             pltpu.VMEM((pair,) + part, bank.dtype),
             pltpu.VMEM((pair,) + part, bank.dtype),
             pltpu.VMEM((pair,) + part, bank.dtype),
-            dma((7, n)),
-            dma((4, n)),
-            dma((4, n)),
-            dma((n,)),
+            dma((7, n, S)),
+            dma((4, n, S)),
+            dma((4, n, pair)),
+            dma((n, pair)),
             dma((n,)),
             dma((n,)),
             dma((2,)),

time: 152 us -> 146 us (0.961)
  Pallas kernels: 139 us -> 134 us
    pallas_call x1, Pallas kernels: 139 us -> 134 us  [run(): pl.pallas_call(functools.partial(gather_kernel, n, A, B, S, rank), out_sh...]
where the time goes in v3:
time: 146 us; the launch traced here: 144 us
  Pallas kernels  134 us (92%)
  local copies, waits for them, and re-layouts  8.88 us (6%)
    pallas_call x1, Pallas kernels, run(): pl.pallas_call(functools.partial(gather_kernel, n, A, B, S, rank), out_sh...  134 us
    unnamed x11, local copies, waits for them, and re-layouts  3.68 us

profile of v3, /device:TPU:0, one launch (start us, length us, event | category | flops | bytes accessed | tf_op | source)
XLA Modules:
  0.0 143.5 jit_solution(3853443321383544025)
XLA Ops:
  0.0 0.0 copy-start
  0.0 0.9 select_reduce_fusion
  0.9 1.8 %reshape_squeeze.6 = bf16[8,2,512,64]{2,1,0,3:T(2,128)(2,1)S(1)} reshape(bf16[1,8192,64]{1,2,0:T(8,128)(2,1)} %param.11) | data formatting | bytes 2097152 | tf_op jit(solution)/shard_map/reshape;squeeze | solution.py:382
  2.7 1.5 %copy.15 = bf16[8,512,2,64]{1,3,2,0:T(8,128)(2,1)} copy(bf16[8,512,2,64]{1,2,0,3:T(2,128)(2,1)S(1)} %bitcast.20) | data formatting | bytes 2097152 | tf_op jit(solution)/shard_map/transpose | solution.py:382
  4.3 0.0 copy-start.4
  4.3 0.0 copy-start.2
  4.3 0.0 copy-start.3
  4.3 1.8 %copy.17 = bf16[8,512,128]{2,1,0:T(8,128)(2,1)S(1)} copy(bf16[8,512,128]{1,2,0:T(8,128)(2,1)} %bitcast.19) | data formatting | bytes 2097152 | tf_op jit(solution)/shard_map/reshape | solution.py:382
  6.1 0.0 copy-done
  6.1 0.1 pad_maximum_fusion.bank_ref
  6.2 0.0 copy-done.4
  6.3 0.0 copy-done.2
  6.3 0.0 copy-done.3
  6.3 0.0 copy-start.1
  6.3 2.8 %copy-done.1 = bf16[2,192,8192]{2,1,0:T(8,128)(2,1)S(1)} copy-done((bf16[2,192,8192]{2,1,0:T(8,128)(2,1)S(1)}, bf16[2,192,8192]{2,1,0:T(8,128)(2,1)}, u32[]{:S(2)}) %copy-start.1) | copy-done | bytes 6291480
  9.1 133.6 %shard_map.82 = bf16[384,1024]{1,0:T(8,128)(2,1)S(1)} custom-call(s32[4]{0:T(128)S(1)} %get-tuple-element.6.pick_ref, s32[4]{0:T(128)S(1)} %get-tuple-element.5.home_ref, s32[4]{0:T(128)S(1)} %copy-done.3, bf16[1,1024]{1,0:T(2,128)(2,1)S(1)} %reshape.20.bias_ref, bf16[4,256,1024]{2,1,0:T(8,128)(2,1)S(1)} %bitcast.18, ...), custom_call_target="tpu_custom_call" | custom-call | tf_op jit(solution)/shard_map/pallas_call | solution.py:326
  142.6 0.9 copy.21
  (3 shorter events, 0.0 us)
Async XLA Ops:
  0.0 6.1 %copy-start = (bf16[1,64,1024]{2,1,0:T(8,128)(2,1)S(1)}, bf16[1,64,1024]{2,1,0:T(8,128)(2,1)}, u32[]{:S(2)}) copy-start(bf16[1,64,1024]{2,1,0:T(8,128)(2,1)} %param.12) | copy-start | bytes 393220
  4.3 1.9 %copy-start.4 = (bf16[1024]{0:T(1024)(128)(2,1)S(1)}, bf16[1024]{0:T(1024)(128)(2,1)}, u32[]{:S(2)}) copy-start(bf16[1024]{0:T(1024)(128)(2,1)} %param.10) | copy-start | bytes 6148
  4.3 2.0 %copy-start.2 = (bf16[1024,1024]{1,0:T(8,128)(2,1)S(1)}, bf16[1024,1024]{1,0:T(8,128)(2,1)}, u32[]{:S(2)}) copy-start(bf16[1024,1024]{1,0:T(8,128)(2,1)} %param.9) | copy-start | bytes 6291460
  4.3 2.0 %copy-start.3 = (s32[4]{0:T(128)S(1)}, s32[4]{0:T(128)}, u32[]{:S(2)}) copy-start(s32[4]{0:T(128)} %length_ref.1) | copy-start | bytes 52
  6.3 2.8 %copy-start.1 = (bf16[2,192,8192]{2,1,0:T(8,128)(2,1)S(1)}, bf16[2,192,8192]{2,1,0:T(8,128)(2,1)}, u32[]{:S(2)}) copy-start(bf16[2,192,8192]{2,1,0:T(8,128)(2,1)} %param.8) | copy-start | bytes 18874372

commit v4 on v3

--- a/solution.py
+++ b/solution.py
@@ -279,11 +279,10 @@
         projects(d - 2)
     steps(adapters, *range(max(A - 2, 0), A))
     if A > 1:
+        crosses(A - 1)
         projects(A - 2)
     stored.wait()
     shrink()
-    if A > 1:
-        crosses(A - 1)
     projects(A - 1)
 
     for c in range(pair):

time: 146 us -> 144 us (0.986); the launches traced: 144 us -> 143 us
  no operation moved by 1% of the time
where the time goes in v4:
time: 144 us; the launch traced here: 143 us
  Pallas kernels  134 us (93%)
  local copies, waits for them, and re-layouts  8.88 us (6%)
    pallas_call x1, Pallas kernels, run(): pl.pallas_call(functools.partial(gather_kernel, n, A, B, S, rank), out_sh...  134 us
    unnamed x11, local copies, waits for them, and re-layouts  3.68 us

profile of v4, /device:TPU:0, one launch (start us, length us, event | category | flops | bytes accessed | tf_op | source)
XLA Modules:
  0.0 143.5 jit_solution(3494565044244737702)
XLA Ops:
  0.0 0.0 copy-start
  0.0 0.9 select_reduce_fusion
  0.9 1.8 %reshape_squeeze.6 = bf16[8,2,512,64]{2,1,0,3:T(2,128)(2,1)S(1)} reshape(bf16[1,8192,64]{1,2,0:T(8,128)(2,1)} %param.11) | data formatting | bytes 2097152 | tf_op jit(solution)/shard_map/reshape;squeeze | solution.py:381
  2.7 1.5 %copy.15 = bf16[8,512,2,64]{1,3,2,0:T(8,128)(2,1)} copy(bf16[8,512,2,64]{1,2,0,3:T(2,128)(2,1)S(1)} %bitcast.20) | data formatting | bytes 2097152 | tf_op jit(solution)/shard_map/transpose | solution.py:381
  4.3 0.0 copy-start.4
  4.3 0.0 copy-start.2
  4.3 0.0 copy-start.3
  4.3 1.8 %copy.17 = bf16[8,512,128]{2,1,0:T(8,128)(2,1)S(1)} copy(bf16[8,512,128]{1,2,0:T(8,128)(2,1)} %bitcast.19) | data formatting | bytes 2097152 | tf_op jit(solution)/shard_map/reshape | solution.py:381
  6.1 0.0 copy-done
  6.1 0.1 pad_maximum_fusion.bank_ref
  6.2 0.0 copy-done.4
  6.3 0.0 copy-done.2
  6.3 0.0 copy-done.3
  6.3 0.0 copy-start.1
  6.3 2.8 %copy-done.1 = bf16[2,192,8192]{2,1,0:T(8,128)(2,1)S(1)} copy-done((bf16[2,192,8192]{2,1,0:T(8,128)(2,1)S(1)}, bf16[2,192,8192]{2,1,0:T(8,128)(2,1)}, u32[]{:S(2)}) %copy-start.1) | copy-done | bytes 6291480
  9.1 133.5 %shard_map.82 = bf16[384,1024]{1,0:T(8,128)(2,1)S(1)} custom-call(s32[4]{0:T(128)S(1)} %get-tuple-element.6.pick_ref, s32[4]{0:T(128)S(1)} %get-tuple-element.5.home_ref, s32[4]{0:T(128)S(1)} %copy-done.3, bf16[1,1024]{1,0:T(2,128)(2,1)S(1)} %reshape.20.bias_ref, bf16[4,256,1024]{2,1,0:T(8,128)(2,1)S(1)} %bitcast.18, ...), custom_call_target="tpu_custom_call" | custom-call | tf_op jit(solution)/shard_map/pallas_call | solution.py:325
  142.6 0.9 copy.21
  (3 shorter events, 0.0 us)
Async XLA Ops:
  0.0 6.1 %copy-start = (bf16[1,64,1024]{2,1,0:T(8,128)(2,1)S(1)}, bf16[1,64,1024]{2,1,0:T(8,128)(2,1)}, u32[]{:S(2)}) copy-start(bf16[1,64,1024]{2,1,0:T(8,128)(2,1)} %param.12) | copy-start | bytes 393220
  4.3 1.9 %copy-start.4 = (bf16[1024]{0:T(1024)(128)(2,1)S(1)}, bf16[1024]{0:T(1024)(128)(2,1)}, u32[]{:S(2)}) copy-start(bf16[1024]{0:T(1024)(128)(2,1)} %param.10) | copy-start | bytes 6148
  4.3 2.0 %copy-start.2 = (bf16[1024,1024]{1,0:T(8,128)(2,1)S(1)}, bf16[1024,1024]{1,0:T(8,128)(2,1)}, u32[]{:S(2)}) copy-start(bf16[1024,1024]{1,0:T(8,128)(2,1)} %param.9) | copy-start | bytes 6291460
  4.3 2.0 %copy-start.3 = (s32[4]{0:T(128)S(1)}, s32[4]{0:T(128)}, u32[]{:S(2)}) copy-start(s32[4]{0:T(128)} %length_ref.1) | copy-start | bytes 52
  6.3 2.8 %copy-start.1 = (bf16[2,192,8192]{2,1,0:T(8,128)(2,1)S(1)}, bf16[2,192,8192]{2,1,0:T(8,128)(2,1)}, u32[]{:S(2)}) copy-start(bf16[2,192,8192]{2,1,0:T(8,128)(2,1)} %param.8) | copy-start | bytes 18874372
